TPU v7x, 32 devices: a whole 2x2x4 slice. The times are simulated.
32 devices in a mesh: freq: 4 (over z), space: 8 (over y, x, core).
Axes of the slice: x: 2, y: 2, z: 4, core: 2. Of those that a mesh axis runs over, the one named last changes fastest.
Arguments:
- wavefields: float32 [2, 4, 2, 2048, 2048], P(None, 'freq', None, 'space'), may hold values from -6 to 6
- frequencies: float32 [4], P('freq'), may hold values from 1.5 to 4
- velocity: float32 [16, 2048, 2048], P('freq', 'space'), may hold values from 1 to 2
- slab_owner: int32 [1], replicated, may hold values from 0 to 15
- ref_velocity: float32 [1, 2], replicated, may hold values from 1 to 2
- ref_index: int32 [1, 128], replicated, may hold values from 0 to 1
Outputs:
- extrapolated: float32 [2, 4, 2, 2048, 2048], P(None, 'freq', None, 'space')
- image: float32 [1, 2048, 2048], P(None, 'space')
All inputs are finite; a program needn't handle non-finite values.
Results may differ from a plain program's by a relative error of at most 0.0003.
Values sent between devices are 32-bit elements; how exact they have to be, the bound alone decides.
A program may use at most 128 MiB of HBM per device.

v0:
```python
import math

import jax
import jax.numpy as jnp
from jax import lax
from jax.sharding import PartitionSpec as P

DZ = 4


def broadcast(value, axis, source):
    kept = jnp.where(lax.axis_index(axis) == source, value, 0).astype(value.dtype)
    return lax.psum(kept, axis)


def extended(cells, sides, width):
    for axis, dim in sides:
        count = lax.axis_size(axis)
        ends = count - 1
        head = lax.slice_in_dim(cells, 0, width, axis=dim)
        tail = lax.slice_in_dim(cells, cells.shape[dim] - width, cells.shape[dim], axis=dim)
        cells = jnp.concatenate(
            [
                lax.ppermute(tail, axis, [(i, (i + 1) % count) for i in range(ends)]),
                cells,
                lax.ppermute(head, axis, [((i + 1) % count, i) for i in range(ends)]),
            ],
            axis=dim,
        )
    return cells


def split_length(length):
    first_len = math.gcd(length, 64)
    return (first_len, length // first_len)


def dft_block(order_size, direction):
    counter = jnp.arange(order_size, dtype=jnp.int32)
    product = counter[:, None] * counter[None, :] % order_size
    phase_angle = direction * 2.0 * math.pi / order_size * product.astype(jnp.float32)
    real_part = jnp.cos(phase_angle)
    imag_part = jnp.sin(phase_angle)
    upper_rows = jnp.stack([real_part, -imag_part], axis=1)
    lower_rows = jnp.stack([imag_part, real_part], axis=1)
    return jnp.stack([upper_rows, lower_rows], axis=0)


def twiddle(first_len, second_len, direction, factor):
    row_numbers = jnp.arange(first_len, dtype=jnp.int32)
    col_numbers = jnp.arange(second_len, dtype=jnp.int32)
    length = first_len * second_len
    product = row_numbers[:, None] * col_numbers[None, :] % length
    phase_angle = direction * 2.0 * math.pi / length * product.astype(jnp.float32)
    return (jnp.cos(phase_angle) * factor, jnp.sin(phase_angle) * factor)


def rotate(values, cosine, sine_part, part_axis):
    position = values.ndim + part_axis
    real_part = lax.index_in_dim(values, 0, position, keepdims=False)
    imag_part = lax.index_in_dim(values, 1, position, keepdims=False)
    return jnp.stack(
        [real_part * cosine - imag_part * sine_part, real_part * sine_part + imag_part * cosine],
        axis=position,
    )


def contract(pattern, matrix, values):
    return jnp.einsum(pattern, matrix, values, precision=lax.Precision.HIGHEST)


def forward_rows(values):
    leading = values.shape[:-3]
    rows_n, length = (values.shape[-2], values.shape[-1])
    first_len, second_len = split_length(length)
    shaped = values.reshape(leading + (2, rows_n, first_len, second_len))
    sectioned = contract("dkca,...crab->...drkb", dft_block(first_len, -1.0), shaped)
    cosine, sine_part = twiddle(first_len, second_len, -1.0, 1.0)
    sectioned = rotate(sectioned, cosine, sine_part, -4)
    sectioned = contract("dqcb,...crkb->...drkq", dft_block(second_len, -1.0), sectioned)
    return sectioned.reshape(leading + (2, rows_n, length))


def forward_cols(values):
    leading = values.shape[:-3]
    length, cols_n = (values.shape[-2], values.shape[-1])
    first_len, second_len = split_length(length)
    shaped = values.reshape(leading + (2, first_len, second_len, cols_n))
    sectioned = contract("dkca,...cabj->...dkbj", dft_block(first_len, -1.0), shaped)
    cosine, sine_part = twiddle(first_len, second_len, -1.0, 1.0)
    sectioned = rotate(sectioned, cosine[:, :, None], sine_part[:, :, None], -4)
    sectioned = contract("dqcb,...ckbj->...djkq", dft_block(second_len, -1.0), sectioned)
    return sectioned.reshape(leading + (2, cols_n, length))


def inverse_cols(values):
    leading = values.shape[:-3]
    cols_n, length = (values.shape[-2], values.shape[-1])
    first_len, second_len = split_length(length)
    shaped = values.reshape(leading + (2, cols_n, first_len, second_len))
    sectioned = contract("dbcq,...cjkq->...djkb", dft_block(second_len, 1.0), shaped)
    cosine, sine_part = twiddle(first_len, second_len, 1.0, 1.0 / length)
    sectioned = rotate(sectioned, cosine, sine_part, -4)
    sectioned = contract("dack,...cjkb->...djab", dft_block(first_len, 1.0), sectioned)
    return sectioned.reshape(leading + (2, cols_n, length))


def inverse_rows(values):
    leading = values.shape[:-3]
    length, rows_n = (values.shape[-2], values.shape[-1])
    first_len, second_len = split_length(length)
    shaped = values.reshape(leading + (2, first_len, second_len, rows_n))
    sectioned = contract("dbcq,...ckqr->...dkbr", dft_block(second_len, 1.0), shaped)
    cosine, sine_part = twiddle(first_len, second_len, 1.0, 1.0 / length)
    sectioned = rotate(sectioned, cosine[:, :, None], sine_part[:, :, None], -4)
    sectioned = contract("dack,...ckbr->...drab", dft_block(first_len, 1.0), sectioned)
    return sectioned.reshape(leading + (2, rows_n, length))


def wave_values(positions, length):
    first_len, second_len = split_length(length)
    natural_order = positions // second_len + first_len * (positions % second_len)
    signed = jnp.where(natural_order < length // 2, natural_order, natural_order - length)
    return 2.0 * math.pi / length * signed.astype(jnp.float32)


def per_device(wavefields, frequencies, velocity, slab_owner, ref_velocity, ref_index):
    field_signs = jnp.array([-1.0, 1.0], dtype=jnp.float32)[:, None, None, None]
    rows_n = wavefields.shape[3]
    width_y = wavefields.shape[4]
    space_count = lax.axis_size("space")
    space_index = lax.axis_index("space")
    width_x = rows_n * space_count
    cols_n = width_y // space_count
    slab_local = velocity.shape[0]
    ky_values = wave_values(space_index * cols_n + jnp.arange(cols_n, dtype=jnp.int32), width_y)
    kx_values = wave_values(jnp.arange(width_x, dtype=jnp.int32), width_x)
    squared = ky_values[:, None] ** 2 + kx_values[None, :] ** 2
    ref_count = ref_velocity.shape[1]
    ref_slots = jnp.arange(ref_count, dtype=jnp.int32)
    fields = wavefields
    owner = slab_owner[0]
    stored = lax.dynamic_index_in_dim(velocity, owner % slab_local, 0, keepdims=False)
    slab_speed = broadcast(stored, "freq", owner // slab_local)
    block_refs = ref_index[0]
    block_count = block_refs.shape[0]
    row_refs = jnp.broadcast_to(block_refs[:, None], (block_count, width_x // block_count)).reshape(
        width_x
    )
    local_refs = lax.dynamic_slice_in_dim(row_refs, space_index * rows_n, rows_n)
    local_masks = (local_refs[None, :] == ref_slots[:, None]).astype(jnp.float32)
    ref_rows = jnp.sum(local_masks * ref_velocity[0][:, None], axis=0)
    spectrum = forward_rows(fields)
    spectrum = lax.all_to_all(spectrum, "space", split_axis=4, concat_axis=3, tiled=True)
    spectrum = forward_cols(spectrum)
    shifted = []
    for ref_slot in range(ref_count):
        vertical = (frequencies[:, None, None] / ref_velocity[0, ref_slot]) ** 2 - squared[None]
        vertical_root = jnp.sqrt(jnp.abs(vertical))
        propagating = vertical >= 0.0
        cosine = jnp.where(propagating, jnp.cos(DZ * vertical_root), jnp.exp(-DZ * vertical_root))
        sine_part = jnp.where(propagating, jnp.sin(DZ * vertical_root), 0.0)
        shifted.append(rotate(spectrum, cosine[None], field_signs * sine_part[None], -3))
    shifted = jnp.stack(shifted, axis=0)
    returned = inverse_cols(shifted)
    ref_masks = (row_refs[None, :] == ref_slots[:, None]).astype(jnp.float32)
    picked = jnp.sum(ref_masks[:, None, None, None, None, :] * returned, axis=0)
    picked = lax.all_to_all(picked, "space", split_axis=4, concat_axis=3, tiled=True)
    wave_now = inverse_rows(picked)
    time_shift = (
        frequencies[:, None, None] * DZ * (1.0 / slab_speed[None] - 1.0 / ref_rows[None, :, None])
    )
    wave_now = rotate(
        wave_now, jnp.cos(time_shift)[None], field_signs * jnp.sin(time_shift)[None], -3
    )
    coupling = (
        DZ
        * (slab_speed[None] - ref_rows[None, :, None])
        * ref_rows[None, :, None]
        / (16.0 * frequencies[:, None, None])
    )
    padded = extended(wave_now, (("space", 3),), 1)
    padded = jnp.pad(padded, ((0, 0), (0, 0), (0, 0), (0, 0), (1, 1)))
    laplace = (
        padded[..., 2:, 1:-1]
        + padded[..., :-2, 1:-1]
        + padded[..., 1:-1, 2:]
        + padded[..., 1:-1, :-2]
        - 4.0 * wave_now
    )
    scaled = field_signs * coupling[None]
    fields = jnp.stack(
        [
            wave_now[:, :, 0] - scaled * laplace[:, :, 1],
            wave_now[:, :, 1] + scaled * laplace[:, :, 0],
        ],
        axis=2,
    )
    local_image = jnp.sum(
        fields[0, :, 0] * fields[1, :, 0] + fields[0, :, 1] * fields[1, :, 1], axis=0
    )
    images = [lax.psum(local_image, "freq")]
    return (fields, jnp.stack(images, axis=0))


def solution(mesh):
    in_specs = (
        P(None, "freq", None, "space", None),
        P("freq"),
        P("freq", "space", None),
        P(),
        P(),
        P(),
    )
    out_specs = (P(None, "freq", None, "space", None), P(None, "space", None))
    return jax.shard_map(
        per_device, mesh=mesh, in_specs=in_specs, out_specs=out_specs, check_vma=False
    )
```

profile of v0, /device:TPU:0, one launch (start us, length us, event | category | flops | bytes accessed | tf_op | source)
XLA Modules:
  0.0 647.9 jit_solution(6611050045300770483)
XLA Ops:
  7.7 8.7 %copy.147 = f32[2,1,2,256,2048]{3,4,2,0,1:T(8,128)} copy(f32[2,1,2,256,2048]{4,3,2,1,0:T(8,128)} %param.7) | data formatting | bytes 16777216 | tf_op args[0]
  16.4 15.6 %fusion.57 = f32[2,1,2,256,64,32]{3,4,5,0,2,1:T(8,128)S(1)} fusion(f32[2,2,256,64,32]{2,4,3,1,0:T(8,128)} %bitcast.225, f32[1,64,2,64]{3,1,2,0:T(8,128)S(1)} %get-tuple-element.40, f32[1,64,2,64]{3,1,2,0:T(8,128)S(1)} %get-tuple-element.39), kind=kOutput, calls=%fused_computation.93 | convolution fusion | flops 3221241856 | bytes 16842752 | tf_op jit(solution)/shard_map/dkca,...crab->...drkb/dot_general | solution.py:69
  34.5 13.8 %fusion.42 = f32[2,1,2,256,64,32]{3,5,2,4,0,1:T(8,128)S(1)} fusion(f32[2,2,256,64,32,1]{2,3,4,0,1,5:T(8,128)S(1)} %maximum_bitcast_fusion.1, f32[1,32,2,32]{3,1,2,0:T(8,128)S(1)} %get-tuple-element.44, f32[1,32,2,32]{3,1,2,0:T(8,128)S(1)} %get-tuple-element.43), kind=kOutput, calls=%fused_computation.88 | convolution fusion | flops 1610616832 | bytes 16793600 | tf_op jit(solution)/shard_map/dqcb,...crkb->...drkq/dot_general | solution.py:69
  50.0 16.5 %copy.151 = f32[2,1,2,256,2048]{3,2,0,1,4:T(2,128)} copy(f32[2,1,2,256,2048]{3,4,2,0,1:T(8,128)S(1)} %bitcast.226) | data formatting | bytes 16777216 | tf_op jit(solution)/shard_map/reshape | solution.py:81
  66.5 5.3 all-to-all-start
  76.8 20.0 %fusion.77 = (f32[256,2048]{0,1:T(8,128)S(1)}, f32[256,2048]{0,1:T(8,128)}, f32[256,2048]{0,1:T(8,128)}, f32[256,2048]{0,1:T(8,128)}) fusion(f32[2048]{0:T(1024)S(1)} %fusion.119, f32[256]{0:T(256)S(1)} %fusion.127, f32[]{:T(128)} %bitcast.45, f32[]{:T(128)} %bitcast.48), kind=kLoop, calls=%fused_computation.113 | loop fusion | flops 7864320 | bytes 8397832 | tf_op jit(solution)/shard_map/jit(_where)/select_n | solution.py:161
  96.8 69.7 %all-to-all-done = f32[2,1,2,256,2048]{3,2,0,1,4:T(2,128)} async-done(((f32[2,1,2,256,2048]{3,2,0,1,4:T(2,128)}), f32[2,1,2,256,2048]{3,2,0,1,4:T(2,128)}, u32[]{:S(2)}, u32[]{:S(2)}) %all-to-all-start) | async-done | bytes 8388640 | tf_op jit(solution)/shard_map/all_to_all | solution.py:154
  166.4 8.4 %copy.152 = f32[2,1,2,256,2048]{3,4,2,0,1:T(8,128)} copy(f32[2,1,2,256,2048]{3,2,0,1,4:T(2,128)} %all-to-all-done) | data formatting | bytes 16777216 | tf_op jit(solution)/shard_map/all_to_all | solution.py:154
  174.8 8.8 %copy.153 = f32[2,1,2,8,256,256]{5,4,3,2,0,1:T(8,128)} copy(f32[2,1,2,8,256,256]{4,5,3,2,0,1:T(8,128)} %bitcast.227) | data formatting | bytes 16777216 | tf_op jit(solution)/shard_map/all_to_all | solution.py:154
  183.6 15.4 %fusion.45 = f32[2,1,2,64,32,256]{5,3,2,4,0,1:T(8,128)S(1)} fusion(f32[2,2,64,32,256,1]{4,3,2,1,0,5:T(8,128)} %bitcast.223, f32[1,64,2,64]{3,1,2,0:T(8,128)S(1)} %get-tuple-element.40, f32[1,64,2,64]{3,1,2,0:T(8,128)S(1)} %get-tuple-element.39), kind=kOutput, calls=%fused_computation.89 | convolution fusion | flops 3221241856 | bytes 16842752 | tf_op jit(solution)/shard_map/dkca,...cabj->...dkbj/dot_general | solution.py:69
  201.4 13.6 %fusion.48 = f32[2,1,2,256,64,32]{3,5,2,4,0,1:T(8,128)S(1)} fusion(f32[2,2,64,32,256,1]{4,2,1,3,0,5:T(8,128)S(1)} %maximum_bitcast_fusion.2, f32[1,32,2,32]{3,1,2,0:T(8,128)S(1)} %get-tuple-element.44, f32[1,32,2,32]{3,1,2,0:T(8,128)S(1)} %get-tuple-element.43), kind=kOutput, calls=%fused_computation.90 | convolution fusion | flops 1610616832 | bytes 16793600 | tf_op jit(solution)/shard_map/dqcb,...ckbj->...djkq/dot_general | solution.py:69
  219.3 6.5 fusion.28
  233.8 18.4 %fusion.23 = f32[2,2,1,2,256,64,32]{4,6,3,5,1,0,2:T(8,128)S(1)} fusion(f32[1,32,2,32]{3,1,2,0:T(8,128)S(1)} %get-tuple-element.42, f32[1,32,2,32]{3,1,2,0:T(8,128)S(1)} %get-tuple-element.41, f32[1,2,1,2,256,64,32]{4,6,5,3,1,2,0:T(8,128)} %bitcast.231, f32[1,2,1,2,256,64,32]{4,6,5,3,1,2,0:T(8,128)} %bitcast.230), kind=kOutput, calls=%fused_computation.50 | convolution fusion | flops 3225423872 | bytes 33570816 | tf_op jit(solution)/shard_map/dbcq,...cjkq->...djkb/dot_general | solution.py:69
  252.3 7.1 %multiply_subtract_fusion = (f32[2,2,1,1,256,64,32]{4,6,3,5,1,0,2:T(8,128)}, f32[2,2,1,1,256,64,32]{4,6,3,5,1,0,2:T(8,128)}) fusion(f32[2,2,1,2,256,64,32]{4,6,3,5,1,0,2:T(8,128)S(1)} %fusion.23, f32[64,32]{1,0:T(8,128)S(1)} %copy.160, f32[64,32]{1,0:T(8,128)S(1)} %copy.159), kind=kLoop, calls=%fused_computation.49 | loop fusion | flops 12582912 | bytes 33570816 | tf_op jit(solution)/shard_map/sub | solution.py:63
  259.4 6.6 %maximum_bitcast_fusion = f32[2,2,2,256,64,32,1]{3,5,2,4,1,0,6:T(8,128)S(1)} fusion(f32[2,2,1,1,256,64,32]{4,6,3,5,1,0,2:T(8,128)} %get-tuple-element.15, f32[2,2,1,1,256,64,32]{4,6,3,5,1,0,2:T(8,128)} %get-tuple-element.14), kind=kLoop, calls=%fused_computation.3 | loop fusion | flops 4194304 | bytes 33554432 | tf_op jit(solution)/shard_map/reshape.45
  266.0 26.4 %fusion = f32[2,2,256,64,32]{2,3,1,4,0:T(8,128)S(1)} fusion(f32[2,64,32]{1,2,0:T(8,128)S(1)} %fusion.95, f32[2,2,2,256,64,32,1]{3,5,2,4,1,0,6:T(8,128)S(1)} %maximum_bitcast_fusion, f32[1,64,2,64]{3,1,2,0:T(8,128)S(1)} %get-tuple-element.38, f32[1,64,2,64]{3,1,2,0:T(8,128)S(1)} %get-tuple-element.37), kind=kOutput, calls=%fused_computation.5 | convolution fusion | flops 6448758784 | bytes 25247744 | tf_op jit(solution)/shard_map/dack,...cjkb->...djab/dot_general | solution.py:69
  292.4 4.9 copy.162
  297.2 16.7 %copy.163 = f32[2,1,2,256,2048]{3,2,0,1,4:T(2,128)} copy(f32[2,1,2,256,2048]{3,4,2,0,1:T(8,128)S(1)} %bitcast.228) | data formatting | bytes 16777216 | tf_op jit(solution)/shard_map/reduce_sum | solution.py:167
  313.9 5.0 all-to-all-start.1
  323.2 88.6 %all-reduce.4.cloned.1.call-done = f32[256,2048]{1,0:T(8,128)} async-done(((f32[256,2048]{1,0:T(8,128)}), f32[256,2048]{1,0:T(8,128)}) %all-reduce.4.cloned.1.call-update) | async-done | bytes 2097168 | tf_op jit(solution)/shard_map/psum | solution.py:13
  411.8 10.6 %fusion.87 = (f32[256,2048]{1,0:T(8,128)}, f32[256,2048]{1,0:T(8,128)}, f32[256,2048]{1,0:T(8,128)}) fusion(f32[256]{0:T(256)S(1)} %get-tuple-element.50, f32[256,2048]{1,0:T(8,128)} %all-reduce.4.cloned.1.call-done, f32[]{:T(128)} %bitcast.93, f32[]{:T(128)} %bitcast.100, f32[256]{0:T(256)S(1)} %get-tuple-element.49, f32[256]{0:T(256)S(1)} %fusion.122), kind=kLoop, calls=%fused_computation.130 | loop fusion | flops 3145728 | bytes 8391688 | tf_op jit(solution)/shard_map/cos | solution.py:174
  427.1 8.4 %copy.164 = f32[2,1,2,256,2048]{3,4,2,0,1:T(8,128)} copy(f32[2,1,2,256,2048]{3,2,0,1,4:T(2,128)} %all-to-all-done.1) | data formatting | bytes 16777216 | tf_op jit(solution)/shard_map/all_to_all | solution.py:168
  435.5 8.8 %copy.165 = f32[2,1,2,8,256,256]{5,4,3,2,0,1:T(8,128)} copy(f32[2,1,2,8,256,256]{4,5,3,2,0,1:T(8,128)} %bitcast.229) | data formatting | bytes 16777216 | tf_op jit(solution)/shard_map/all_to_all | solution.py:168
  444.3 9.4 %fusion.51 = f32[2,1,2,64,32,256]{5,4,2,3,0,1:T(8,128)S(1)} fusion(f32[2,2,64,32,256,1]{4,3,2,1,0,5:T(8,128)} %bitcast.222, f32[1,32,2,32]{3,1,2,0:T(8,128)S(1)} %get-tuple-element.42, f32[1,32,2,32]{3,1,2,0:T(8,128)S(1)} %get-tuple-element.41), kind=kOutput, calls=%fused_computation.91 | convolution fusion | flops 1610616832 | bytes 16793600 | tf_op jit(solution)/shard_map/dbcq,...ckqr->...dkbr/dot_general | solution.py:69
  456.8 13.6 %fusion.54 = f32[2,1,2,256,64,32]{3,4,2,5,0,1:T(8,128)S(1)} fusion(f32[2,2,64,32,256,1]{4,3,1,2,0,5:T(8,128)S(1)} %maximum_bitcast_fusion.3, f32[1,64,2,64]{3,1,2,0:T(8,128)S(1)} %get-tuple-element.38, f32[1,64,2,64]{3,1,2,0:T(8,128)S(1)} %get-tuple-element.37), kind=kOutput, calls=%fused_computation.92 | convolution fusion | flops 3221241856 | bytes 16842752 | tf_op jit(solution)/shard_map/dack,...ckbr->...drab/dot_general | solution.py:69
  501.5 15.5 %select_maximum_fusion = f32[2,1,2,258,2050]{3,4,0,2,1:T(8,128)} fusion(f32[2,1,2,1,2048]{3,4,0,2,1:T(8,128)} %copy.178, f32[2,1,2,1,2048]{3,4,0,2,1:T(8,128)} %copy.180, f32[2,1,1,256,2048]{3,4,0,2,1:T(8,128)} %copy-done.2, f32[2,1,1,256,2048]{3,4,0,2,1:T(8,128)} %copy-done), kind=kLoop, calls=%fused_computation.11 | loop fusion | flops 21156000 | bytes 16916544 | tf_op jit(solution)/shard_map/concatenate | solution.py:22
  517.0 22.9 %fusion.8 = f32[2,1,2,256,2048]{3,4,0,2,1:T(8,128)} fusion(f32[2,1,1,256,2048]{3,4,0,2,1:T(8,128)} %copy-done.2, f32[2,1,1,256,2048]{3,4,0,2,1:T(8,128)S(1)} %copy-done.1, f32[2,1,2,258,2050]{3,4,0,2,1:T(8,128)} %select_maximum_fusion, f32[2,1,2,1,2048]{3,4,0,2,1:T(8,128)} %copy.180, f32[2,1,2,1,2048]{3,4,0,2,1:T(8,128)} %copy.178), kind=kLoop, calls=%fused_computation.21 | loop fusion | flops 20971520 | bytes 33619968 | tf_op jit(solution)/shard_map/sub | solution.py:185
  539.9 7.9 %fusion.35 = (f32[2,1,256,2048]{2,3,0,1:T(8,128)S(1)}, f32[2,1,256,2048]{2,3,0,1:T(8,128)S(1)}) fusion(f32[2,1,2,256,2048]{3,4,0,2,1:T(8,128)} %fusion.8, f32[2,1,2,256,2048]{3,4,2,0,1:T(8,128)} %bitcast.221, f32[256,2048]{0,1:T(8,128)} %copy.176, f32[256,2048]{0,1:T(8,128)} %copy.174, f32[2]{0:T(128)S(1)} %copy-done.6, f32[256,2048]{0,1:T(8,128)S(1)} %copy.172), kind=kLoop, calls=%fused_computation.68 | loop fusion | flops 12582912 | bytes 31457288 | tf_op jit(solution)/shard_map/sub | solution.py:194
  549.8 10.5 %fusion.32 = (f32[2,1,1,256,2048]{3,4,2,0,1:T(8,128)}, f32[2,1,1,256,2048]{3,4,2,0,1:T(8,128)}) fusion(f32[2,1,1,256,2048]{3,4,0,2,1:T(8,128)} %copy-done, f32[2,1,2,256,2048]{3,4,0,2,1:T(8,128)} %fusion.8, f32[256,2048]{0,1:T(8,128)S(1)} %copy-done.5, f32[2]{0:T(128)S(1)} %copy-done.6, f32[2,1,1,256,2048]{3,4,0,2,1:T(8,128)} %copy-done.2), kind=kLoop, calls=%fused_computation.65 | loop fusion | flops 5242880 | bytes 27262984 | tf_op jit(solution)/shard_map/sub | solution.py:194
  560.3 7.3 %pad_maximum_fusion.8 = f32[2,1,2,256,2048]{3,4,2,0,1:T(8,128)} fusion(f32[2,1,1,256,2048]{3,4,2,0,1:T(8,128)} %get-tuple-element.23, f32[2,1,1,256,2048]{3,4,2,0,1:T(8,128)} %get-tuple-element.22), kind=kLoop, calls=%fused_computation.34 | loop fusion | flops 2097152 | bytes 16777216 | tf_op jit(solution)/shard_map/stack | solution.py:192
  567.6 8.7 %copy.190 = f32[2,1,2,256,2048]{4,3,2,1,0:T(8,128)} copy(f32[2,1,2,256,2048]{3,4,2,0,1:T(8,128)} %pad_maximum_fusion.8) | data formatting | bytes 16777216
  576.3 61.7 %all-reduce.6.cloned.1.call-done = f32[1,256,2048]{1,2,0:T(8,128)} async-done(((f32[1,256,2048]{1,2,0:T(8,128)}), f32[1,256,2048]{1,2,0:T(8,128)}) %all-reduce.6.cloned.1.call-update) | async-done | bytes 2097168 | tf_op jit(solution)/shard_map/psum | solution.py:202
  (81 shorter events, 69.5 us)
Async XLA Ops:
  66.5 6.0 copy-start.7
  66.5 8.8 %copy-start.8 = (s32[1,128]{1,0:T(1,128)S(1)}, s32[1,128]{1,0:T(1,128)}, u32[]{:S(2)}) copy-start(s32[1,128]{1,0:T(1,128)} %param.12) | copy-start | bytes 1540
  66.5 99.9 %all-to-all-start = ((f32[2,1,2,256,2048]{3,2,0,1,4:T(2,128)}), f32[2,1,2,256,2048]{3,2,0,1,4:T(2,128)}, u32[]{:S(2)}, u32[]{:S(2)}) async-start(f32[2,1,2,256,2048]{3,2,0,1,4:T(2,128)} %copy.151), calls=%async_computation | async-start | bytes 16777216 | tf_op jit(solution)/shard_map/all_to_all | solution.py:154
  215.0 4.3 copy-start.6
  313.9 113.2 %all-to-all-start.1 = ((f32[2,1,2,256,2048]{3,2,0,1,4:T(2,128)}), f32[2,1,2,256,2048]{3,2,0,1,4:T(2,128)}, u32[]{:S(2)}, u32[]{:S(2)}) async-start(f32[2,1,2,256,2048]{3,2,0,1,4:T(2,128)} %copy.163), calls=%async_computation.1 | async-start | bytes 16777216 | tf_op jit(solution)/shard_map/all_to_all | solution.py:168
  318.9 92.9 %all-reduce.4.cloned.1.call-start = ((), (), s32[]{:S(2)}) async-start(), calls=%async_computation.2 | async-start | bytes 4194304 | tf_op jit(solution)/shard_map/psum | solution.py:13
  322.8 315.2 %all-reduce.6.cloned.1.call-start = ((), (), s32[]{:S(2)}) async-start(), calls=%async_computation.3 | async-start | bytes 4194304 | tf_op jit(solution)/shard_map/psum | solution.py:202
  470.4 4.9 copy-start.4
  475.2 3.2 copy-start.3
  478.4 4.6 copy-start
  478.4 5.8 copy-start.2
  487.1 9.0 %collective-permute-start.1 = (f32[2,1,2,1,2048]{4,2,3,1,0:T(2,128)S(1)}, f32[2,1,2,1,2048]{4,2,3,1,0:T(2,128)S(1)}, u32[]{:S(2)}, u32[]{:S(2)}) collective-permute-start(f32[2,1,2,1,2048]{4,2,3,1,0:T(2,128)S(1)} %copy.179), channel_id=1, source_target_pairs={{0,1},{1,2},{2,3},{3,4},{4,5},{5,6},{6,7},{8,9},{9,10},{10,11},{11... | collective-permute-start | bytes 98312 | tf_op jit(solution)/shard_map/ppermute | solution.py:24
  491.7 7.1 %collective-permute-start = (f32[2,1,2,1,2048]{4,2,3,1,0:T(2,128)S(1)}, f32[2,1,2,1,2048]{4,2,3,1,0:T(2,128)S(1)}, u32[]{:S(2)}, u32[]{:S(2)}) collective-permute-start(f32[2,1,2,1,2048]{4,2,3,1,0:T(2,128)S(1)} %copy.177), channel_id=1, source_target_pairs={{1,0},{2,1},{3,2},{4,3},{5,4},{6,5},{7,6},{9,8},{10,9},{11,10},{12... | collective-permute-start | bytes 98312 | tf_op jit(solution)/shard_map/ppermute | solution.py:26
  501.5 15.5 %copy-start.1 = (f32[2,1,1,256,2048]{3,4,0,2,1:T(8,128)S(1)}, f32[2,1,1,256,2048]{3,4,0,2,1:T(8,128)}, u32[]{:S(2)}) copy-start(f32[2,1,1,256,2048]{3,4,0,2,1:T(8,128)} %copy-done) | copy-start | bytes 12582916
  547.9 1.9 copy-start.5
Sparse Core Ops, SparseCore 0:
  322.9 88.8 all-reduce.3
  549.9 88.0 all-reduce.5
where the time goes:
time: 655 us; the launch traced here: 648 us
  waiting for transfers between devices  220 us (34%)
  other arithmetic  144 us (22%)
  local copies, waits for them, and re-layouts  127 us (19%)
  matrix products  126 us (19%)
  between operations  17.3 us (3%)
  starting transfers between devices  13.4 us (2%)
    dot_general x8, matrix products, contract(): return jnp.einsum(pattern, matrix, values, precision=lax.Precision.HIGHEST)  126 us
    psum x1, waiting for transfers between devices, broadcast(): return lax.psum(kept, axis)  88.6 us
    all_to_all x1, waiting for transfers between devices, per_device(): lax.all_to_all(spectrum, 'space', split_axis=4, concat_axis=3, tiled=True)  69.7 us
    psum x1, waiting for transfers between devices, per_device(): images = [lax.psum(local_image, 'freq')]  61.7 us
    unnamed x22, local copies, waits for them, and re-layouts  24 us
    sub x1, other arithmetic, per_device(): padded[..., 2:, 1:-1] + padded[..., :-2, 1:-1] + padded[..., 1:-1, 2:]  22.9 us
    reduce_sum x2, local copies, waits for them, and re-layouts, per_device(): picked = jnp.sum(ref_masks[:, None, None, None, None, :] * returned, axis=0)  21.5 us
    select_n x1, other arithmetic, per_device(): jnp.where(propagating, jnp.cos(DZ * vertical_root), jnp.exp(-DZ * vertica...  20 us
  transfers between devices with their start and end apart: 6, of which 3 were waited for; matrix products, arithmetic and copies ran while one was open for 12% of the time, Pallas kernels for 0%

commit v1 on v0

v1 whole, which is shorter than its diff:
```python
import functools
import math

import jax
import jax.numpy as jnp
import ml_dtypes
import numpy as np
from jax import lax
from jax.experimental import pallas as pl
from jax.experimental.pallas import tpu as pltpu
from jax.sharding import PartitionSpec as P

DZ = 4
LANES = 128
GROUP = 8
LIMIT = 56 * 1024 * 1024


def short_transform(values, direction):
    count = len(values)
    if count == 1:
        return values
    even = short_transform(values[0::2], direction)
    odd = short_transform(values[1::2], direction)
    low, high = [], []
    for k in range(count // 2):
        er, ei = even[k]
        orr, oi = odd[k]
        if k == 0:
            tr, ti = orr, oi
        elif 4 * k == count:
            tr, ti = (oi, -orr) if direction < 0 else (-oi, orr)
        else:
            c = math.cos(2.0 * math.pi * k / count)
            s = direction * math.sin(2.0 * math.pi * k / count)
            tr, ti = orr * c - oi * s, orr * s + oi * c
        low.append((er + tr, ei + ti))
        high.append((er - tr, ei - ti))
    return low + high


def halves(matrix):
    upper = matrix.astype(np.float32).astype(ml_dtypes.bfloat16)
    lower = (matrix - upper.astype(np.float64)).astype(ml_dtypes.bfloat16)
    return np.stack([upper, lower])


def block_matrix(direction, factor, left):
    index = np.arange(LANES)
    angle = direction * 2.0 * np.pi / LANES * (index[:, None] * index[None, :] % LANES)
    c, s = np.cos(angle) * factor, np.sin(angle) * factor
    matrix = np.block([[c, -s], [s, c]])
    return halves(matrix if left else matrix.T)


def twiddles(outer, spread):
    length = outer * LANES
    product = np.arange(outer)[:, None] * np.arange(LANES)[None, :] % length
    angle = -2.0 * np.pi / length * product
    table = np.stack([np.cos(angle), np.sin(angle)], axis=1).astype(np.float32)
    if spread:
        return np.ascontiguousarray(np.broadcast_to(table[..., None], table.shape + (spread,)))
    return table[:, :, None, :]


def split(values):
    upper = values.astype(jnp.bfloat16)
    return upper, (values - upper.astype(jnp.float32)).astype(jnp.bfloat16)


def dot(a, b):
    return jnp.dot(a, b, preferred_element_type=jnp.float32)


def times_right(values, matrix):
    upper, lower = split(values)
    return dot(upper, matrix[0]) + (dot(lower, matrix[0]) + dot(upper, matrix[1]))


def times_left(matrix, values):
    upper, lower = split(values)
    return dot(matrix[0], upper) + (dot(matrix[0], lower) + dot(matrix[1], upper))


def turn(value, c, s):
    return value[0] * c - value[1] * s, value[0] * s + value[1] * c


def rows_kernel(outer, cols_n, fields, table, matrix, out, scratch):
    rows = fields.shape[3]

    def group(i, carry):
        at = pl.ds(pl.multiple_of(i * GROUP, GROUP), GROUP)
        values = [
            tuple(fields[0, 0, c, at, a * LANES : (a + 1) * LANES] for c in range(2))
            for a in range(outer)
        ]
        values = short_transform(values, -1.0)
        for k, value in enumerate(values):
            re, im = turn(value, table[k, 0], table[k, 1]) if k else value
            scratch[k, at, :LANES] = re
            scratch[k, at, LANES:] = im
        return carry

    lax.fori_loop(0, rows // GROUP, group, 0)
    width = min(cols_n, LANES)
    for k in range(outer):
        both = times_right(scratch[k], matrix)
        for q in range(LANES // width):
            column = k * LANES + q * width
            dest, off = column // cols_n, column % cols_n
            for c in range(2):
                begin = c * LANES + q * width
                out[dest, c, :, off : off + width] = both[:, begin : begin + width]


def forward_rows(wavefields, j, space, cols_n):
    rows_n, length = wavefields.shape[3:]
    outer = length // LANES
    rows = math.gcd(rows_n, 64)
    whole = lambda *shape: pl.BlockSpec(shape, lambda i: (0,) * len(shape))
    return pl.pallas_call(
        functools.partial(rows_kernel, outer, cols_n),
        grid=(rows_n // rows,),
        in_specs=[
            pl.BlockSpec((1, 1, 2, rows, length), lambda i: (j, 0, 0, i, 0)),
            whole(outer, 2, 1, LANES),
            whole(2, 256, 256),
        ],
        out_specs=pl.BlockSpec((space, 2, rows, cols_n), lambda i: (0, 0, i, 0)),
        out_shape=jax.ShapeDtypeStruct((space, 2, rows_n, cols_n), jnp.float32),
        scratch_shapes=[pltpu.VMEM((outer, rows, 2 * LANES), jnp.float32)],
        compiler_params=pltpu.CompilerParams(vmem_limit_bytes=LIMIT),
        cost_estimate=pl.CostEstimate(
            flops=rows_n * length * 6000, bytes_accessed=rows_n * length * 16, transcendentals=0
        ),
    )(wavefields, jnp.asarray(twiddles(outer, 0)), jnp.asarray(block_matrix(-1.0, 1.0, False)))


def middle_kernel(outer, sign, rows_n, chunks, per_ref, *refs):
    chosen, fields, phase, table, forward, inverse = refs[:6]
    outs = refs[6 : 6 + chunks]
    spectrum, returned = refs[6 + chunks :]
    ref_count = phase.shape[0]
    part = rows_n // chunks
    lanes = fields.shape[3]

    def place(a, i):
        if rows_n >= LANES:
            return a * LANES // rows_n, a * LANES % rows_n, i * GROUP
        per = LANES // rows_n
        return a * per + i * GROUP // rows_n, 0, lax.rem(i * GROUP, rows_n)

    def first(i, carry):
        at = pl.multiple_of(i * GROUP, GROUP)
        values = []
        for a in range(outer):
            src, base, shift = place(a, i)
            row = pl.ds(pl.multiple_of(base + shift, GROUP), GROUP)
            values.append(tuple(fields[src, c, row, :] for c in range(2)))
        values = short_transform(values, -1.0)
        for k, value in enumerate(values):
            row = pl.ds(at, GROUP)
            if k:
                value = turn(value, table[k, 0, row, :], table[k, 1, row, :])
            for c in range(2):
                spectrum[k, pl.ds(at + c * LANES, GROUP), :] = value[c]
        return carry

    lax.fori_loop(0, LANES // GROUP, first, 0)

    def second(k, carry):
        both = times_left(forward, spectrum[k])
        re, im = both[:LANES], both[LANES:]
        for r in range(ref_count):
            shifted = turn((re, im), phase[r, 0, k], sign * phase[r, 1, k])
            returned[r, k] = times_left(inverse, jnp.concatenate(shifted, axis=0))
        return carry

    lax.fori_loop(0, outer, second, 0)

    def third(i, carry):
        at = pl.multiple_of(i * GROUP, GROUP)
        row = pl.ds(at, GROUP)
        for r in range(ref_count):
            values = []
            for k in range(outer):
                value = tuple(returned[r, k, pl.ds(at + c * LANES, GROUP), :] for c in range(2))
                if k:
                    value = turn(value, table[k, 0, row, :], -table[k, 1, row, :])
                values.append(value)
            values = short_transform(values, 1.0)
            for a, value in enumerate(values):
                src, base, shift = place(a, i)
                out = outs[base // part]
                target = pl.ds(pl.multiple_of(base % part + shift, GROUP), GROUP)
                for c in range(2):
                    if r:
                        mine = chosen[(a * LANES + i * GROUP) // per_ref] == r
                        kept = jnp.where(mine, value[c], out[src, c, target, :])
                    else:
                        kept = value[c]
                    out[src, c, target, :] = kept
        return carry

    lax.fori_loop(0, LANES // GROUP, third, 0)
    space = fields.shape[0]

    def edges(d, carry):
        for h in range(chunks):
            for side in range(2):
                slot = part + 2 * h + side
                if side == 0:
                    from_h = h - 1 if h else chunks - 1
                    from_d = d if h else jnp.maximum(d - 1, 0)
                    row = part - 1
                else:
                    from_h = h + 1 if h + 1 < chunks else 0
                    from_d = d if h + 1 < chunks else jnp.minimum(d + 1, space - 1)
                    row = 0
                for c in range(2):
                    outs[0][d, c, slot : slot + 1, :] = outs[from_h][from_d, c, row : row + 1, :]
        for c in range(2):
            outs[0][d, c, part + 2 * chunks : part + GROUP, :] = jnp.zeros(
                (GROUP - 2 * chunks, lanes), jnp.float32
            )
        return carry

    lax.fori_loop(0, space, edges, 0)


def middle(spectrum, phase, chosen, sign, chunks):
    space, _, rows_n, cols_n = spectrum.shape
    ref_count = phase.shape[0]
    length = space * rows_n
    outer = length // LANES
    width = math.gcd(cols_n, LANES)
    part = rows_n // chunks
    heights = [part + GROUP * (h == 0) for h in range(chunks)]
    whole = lambda *shape: pl.BlockSpec(shape, lambda i: (0,) * len(shape))
    return pl.pallas_call(
        functools.partial(
            middle_kernel, outer, sign, rows_n, chunks, length // chosen.shape[0]
        ),
        grid=(cols_n // width,),
        in_specs=[
            pl.BlockSpec(memory_space=pltpu.SMEM),
            pl.BlockSpec((space, 2, rows_n, width), lambda i: (0, 0, 0, i)),
            pl.BlockSpec((ref_count, 2, outer, LANES, width), lambda i: (0, 0, 0, 0, i)),
            whole(outer, 2, LANES, width),
            whole(2, 256, 256),
            whole(2, 256, 256),
        ],
        out_specs=[
            pl.BlockSpec((space, 2, height, width), lambda i: (0, 0, 0, i)) for height in heights
        ],
        out_shape=[
            jax.ShapeDtypeStruct((space, 2, height, cols_n), jnp.float32) for height in heights
        ],
        scratch_shapes=[
            pltpu.VMEM((outer, 2 * LANES, width), jnp.float32),
            pltpu.VMEM((ref_count, outer, 2 * LANES, width), jnp.float32),
        ],
        compiler_params=pltpu.CompilerParams(vmem_limit_bytes=LIMIT),
        cost_estimate=pl.CostEstimate(
            flops=length * cols_n * 20000, bytes_accessed=length * cols_n * 32, transcendentals=0
        ),
    )(
        chosen,
        spectrum,
        phase,
        jnp.asarray(twiddles(outer, width)),
        jnp.asarray(block_matrix(-1.0, 1.0, True)),
        jnp.asarray(block_matrix(1.0, 1.0 / length, True)),
    )


def final_kernel(outer, chunk, aliased, part, *refs):
    source, receiver, edge0, edge1, shift, shift_edge, beta, table, inverse = refs[:9]
    out, image = refs[9 + aliased : 11 + aliased]
    lines, wave = refs[11 + aliased :]
    cols_n = source.shape[3]
    width = min(cols_n, LANES)
    length = outer * LANES

    for j, (main, edge) in enumerate(((source, edge0), (receiver, edge1))):
        sign = -1.0 if j == 0 else 1.0

        for k in range(outer):
            pieces = []
            for c in range(2):
                for q in range(LANES // width):
                    column = k * LANES + q * width
                    src, off = column // cols_n, column % cols_n
                    span = slice(off, off + width)
                    pieces.append(
                        jnp.concatenate([main[src, c, :part, span], edge[src, c, :, span]], axis=0)
                    )
            both = times_right(jnp.concatenate(pieces, axis=1), inverse)
            lines[k] = both

        def lines_of(at):
            row = pl.ds(at, GROUP)
            values = []
            for k in range(outer):
                value = (lines[k, row, :LANES], lines[k, row, LANES:])
                if k:
                    value = turn(value, table[k, 0], -table[k, 1])
                values.append(value)
            return short_transform(values, 1.0)

        def group(i, carry):
            at = pl.multiple_of(i * GROUP, GROUP)
            row = pl.ds(at, GROUP)
            values = lines_of(at)
            for a, value in enumerate(values):
                span = slice(a * LANES, (a + 1) * LANES)
                value = turn(value, shift[0, row, span], sign * shift[1, row, span])
                for c in range(2):
                    wave[j, c, pl.ds(at + GROUP, GROUP), span] = value[c]
            return carry

        lax.fori_loop(0, part // GROUP, group, 0)
        values = lines_of(part)
        for a, value in enumerate(values):
            span = slice(a * LANES, (a + 1) * LANES)
            value = turn(value, shift_edge[0, :, span], sign * shift_edge[1, :, span])
            for c in range(2):
                wave[j, c, GROUP - 1 : GROUP, span] = value[c][2 * chunk : 2 * chunk + 1]
                wave[j, c, part + GROUP : part + GROUP + 1, span] = value[c][
                    2 * chunk + 1 : 2 * chunk + 2
                ]

    lane = lax.broadcasted_iota(jnp.int32, (GROUP, length), 1)
    line = lax.broadcasted_iota(jnp.int32, (GROUP, length), 0)

    def stencil(i, carry):
        at = pl.multiple_of(i * GROUP, GROUP)
        row = pl.ds(at, GROUP)
        factor = beta[row, :]
        total = jnp.zeros((GROUP, length), jnp.float32)
        kept = []
        for j in range(2):
            sign = -1.0 if j == 0 else 1.0
            laplace, centre = [], []
            for c in range(2):
                now = wave[j, c, pl.ds(at + GROUP, GROUP), :]
                before = wave[j, c, row, :]
                after = wave[j, c, pl.ds(at + 2 * GROUP, GROUP), :]
                up = jnp.where(line == 0, pltpu.roll(before, 1, 0), pltpu.roll(now, 1, 0))
                down = jnp.where(
                    line == GROUP - 1,
                    pltpu.roll(after, GROUP - 1, 0),
                    pltpu.roll(now, GROUP - 1, 0),
                )
                left = jnp.where(lane == 0, 0.0, pltpu.roll(now, 1, 1))
                right = jnp.where(lane == length - 1, 0.0, pltpu.roll(now, length - 1, 1))
                laplace.append(down + up + right + left - 4.0 * now)
                centre.append(now)
            scaled = sign * factor
            re = centre[0] - scaled * laplace[1]
            im = centre[1] + scaled * laplace[0]
            out[j, 0, 0, row, :] = re
            out[j, 0, 1, row, :] = im
            kept.append((re, im))
        image[row, :] = kept[0][0] * kept[1][0] + kept[0][1] * kept[1][1]
        return carry

    lax.fori_loop(0, part // GROUP, stencil, 0)


def final(main, edge, shift, shift_edge, beta, chunk, chunks, earlier):
    space, _, _, cols_n = main[0].shape
    part = shift.shape[1] // chunks
    length = space * cols_n
    outer = length // LANES
    aliased = int(earlier is not None)
    whole = lambda *shape: pl.BlockSpec(shape, lambda i: (0,) * len(shape))
    edge_spec = pl.BlockSpec((space, 2, GROUP, cols_n), lambda i: (0, 0, part // GROUP, 0))
    main_spec = pl.BlockSpec((space, 2, part, cols_n), lambda i: (0, 0, 0, 0))
    return pl.pallas_call(
        functools.partial(final_kernel, outer, chunk, aliased, part),
        grid=(1,),
        in_specs=[
            main_spec,
            main_spec,
            edge_spec,
            edge_spec,
            pl.BlockSpec((2, part, length), lambda i: (0, chunk, 0)),
            whole(2, GROUP, length),
            pl.BlockSpec((part, length), lambda i: (chunk, 0)),
            whole(outer, 2, 1, LANES),
            whole(2, 256, 256),
        ]
        + [pl.BlockSpec(memory_space=pl.ANY)] * aliased,
        out_specs=[
            pl.BlockSpec((2, 1, 2, part, length), lambda i: (0, 0, 0, chunk, 0)),
            whole(part, length),
        ],
        out_shape=[
            jax.ShapeDtypeStruct((2, 1, 2, part * chunks, length), jnp.float32),
            jax.ShapeDtypeStruct((part, length), jnp.float32),
        ],
        scratch_shapes=[
            pltpu.VMEM((outer, part + GROUP, 2 * LANES), jnp.float32),
            pltpu.VMEM((2, 2, part + 2 * GROUP, length), jnp.float32),
        ],
        input_output_aliases={9: 0} if aliased else {},
        compiler_params=pltpu.CompilerParams(vmem_limit_bytes=LIMIT),
        cost_estimate=pl.CostEstimate(
            flops=part * length * 15000, bytes_accessed=part * length * 60, transcendentals=0
        ),
    )(
        main[0],
        main[1],
        edge[0],
        edge[1],
        shift,
        shift_edge,
        beta,
        jnp.asarray(twiddles(outer, 0)),
        jnp.asarray(block_matrix(1.0, 1.0 / length, False)),
        *([earlier] if aliased else []),
    )


def wave_values(positions, length):
    outer = length // LANES
    natural_order = positions // LANES + outer * (positions % LANES)
    signed = jnp.where(natural_order < length // 2, natural_order, natural_order - length)
    return 2.0 * math.pi / length * signed.astype(jnp.float32)


def per_device(wavefields, frequencies, velocity, slab_owner, ref_velocity, ref_index):
    rows_n, width_y = wavefields.shape[3:]
    space = lax.axis_size("space")
    me = lax.axis_index("space")
    width_x = rows_n * space
    cols_n = width_y // space
    slab_local = velocity.shape[0]
    ref_count = ref_velocity.shape[1]
    chunks = 2 if rows_n >= 2 * LANES else 1
    part = rows_n // chunks
    omega = frequencies[0]

    owner = slab_owner[0]
    stored = lax.dynamic_index_in_dim(velocity, owner % slab_local, 0, keepdims=False)
    stored = jnp.where(lax.axis_index("freq") == owner // slab_local, stored, 0.0)
    speed = lax.psum(stored, "freq")

    swap = lambda x: lax.all_to_all(x, "space", split_axis=0, concat_axis=0, tiled=True)
    spectra = [swap(forward_rows(wavefields, j, space, cols_n)) for j in range(2)]

    ky = wave_values(me * cols_n + jnp.arange(cols_n, dtype=jnp.int32), width_y)
    kx = wave_values(jnp.arange(width_x, dtype=jnp.int32), width_x)
    squared = kx[:, None] ** 2 + ky[None, :] ** 2
    vertical = (omega / ref_velocity[0][:, None, None]) ** 2 - squared[None]
    root = jnp.sqrt(jnp.abs(vertical))
    fits = vertical >= 0.0
    cosine = jnp.where(fits, jnp.cos(DZ * root), jnp.exp(-DZ * root))
    sine = jnp.where(fits, jnp.sin(DZ * root), 0.0)
    phase = jnp.stack([cosine, sine], axis=1).reshape(
        ref_count, 2, width_x // LANES, LANES, cols_n
    )

    count = space
    above = lax.ppermute(speed[-1:], "space", [(i, i + 1) for i in range(count - 1)])
    below = lax.ppermute(speed[:1], "space", [(i + 1, i) for i in range(count - 1)])
    edge_rows, edge_speed = [], []
    for h in range(chunks):
        for local, outside, kept in (
            (h * part - 1, h == 0, above),
            ((h + 1) * part, h == chunks - 1, below),
        ):
            edge_rows.append(local)
            edge_speed.append(kept if outside else speed[local : local + 1])
    while len(edge_rows) < GROUP:
        edge_rows.append(0)
        edge_speed.append(speed[:1])
    block_refs = ref_index[0]
    per_ref = width_x // block_refs.shape[0]

    def shifts(c, rows):
        inside = (rows >= 0) & (rows < width_x)
        cr = ref_velocity[0][block_refs[jnp.clip(rows, 0, width_x - 1) // per_ref]][:, None]
        safe = jnp.where(inside[:, None], c, 1.0)
        angle = omega * DZ * (1.0 / safe - 1.0 / cr)
        keep = inside[:, None].astype(jnp.float32)
        return jnp.stack([jnp.cos(angle) * keep, jnp.sin(angle) * keep]), cr

    start = me * rows_n
    shift, cr = shifts(speed, start + jnp.arange(rows_n, dtype=jnp.int32))
    beta = DZ * (speed - cr) * cr / (16.0 * omega)
    shift_edge, _ = shifts(
        jnp.concatenate(edge_speed, axis=0), start + jnp.array(edge_rows, dtype=jnp.int32)
    )

    moved = []
    for j in range(2):
        moved.append(middle(spectra[j], phase, block_refs, -1.0 if j == 0 else 1.0, chunks))
    back = [[swap(moved[j][h]) for j in range(2)] for h in range(chunks)]
    fields, images = None, []
    for h in range(chunks):
        fields, image = final(back[h], back[0], shift, shift_edge, beta, h, chunks, fields)
        images.append(lax.psum(image, "freq"))
    return fields, jnp.concatenate(images, axis=0)[None]


def solution(mesh):
    in_specs = (
        P(None, "freq", None, "space", None),
        P("freq"),
        P("freq", "space", None),
        P(),
        P(),
        P(),
    )
    out_specs = (P(None, "freq", None, "space", None), P(None, "space", None))
    return jax.shard_map(
        per_device, mesh=mesh, in_specs=in_specs, out_specs=out_specs, check_vma=False
    )
```

time: 655 us -> 405 us (0.62)
  matrix products: 126 us -> 0 us
  local copies, waits for them, and re-layouts: 127 us -> 8.12 us
  Pallas kernels: 0 us -> 105 us
  other arithmetic: 144 us -> 42.9 us
  waiting for transfers between devices: 220 us -> 174 us
  blocking collectives: 0 us -> 30.9 us
  starting transfers between devices: 13.4 us -> 26.9 us
    dot_general x8 -> x0, matrix products: 126 us -> none  [contract(): return jnp.einsum(pattern, matrix, values, precision=lax.Precision.HIGHEST)]
    pallas_call x0 -> x6, Pallas kernels: none -> 105 us  [the longest x2 61.3 us: middle(): pl.pallas_call(functools.partial(middle_kernel, outer, sign, rows_n, chun...]
    sub x9 -> x0, other arithmetic: 60.2 us -> none  [the longest x1 22.9 us: per_device(): padded[..., 2:, 1:-1] + padded[..., :-2, 1:-1] + padded[..., 1:-1, 2:]]
    all_to_all x4 -> x0, local copies, waits for them, and re-layouts: 34.3 us -> none  [the longest x2 17.2 us: per_device(): lax.all_to_all(picked, 'space', split_axis=4, concat_axis=3, tiled=True)]
    all_to_all x0 -> x1, blocking collectives: none -> 30.9 us  [per_device(): lax.all_to_all(x, 'space', split_axis=0, concat_axis=0, tiled=True)]
    all_to_all x2 -> x5, waiting for transfers between devices: 69.7 us -> 40.6 us  [per_device(): lax.all_to_all(x, 'space', split_axis=0, concat_axis=0, tiled=True)]
    reduce_sum x2 -> x0, local copies, waits for them, and re-layouts: 21.5 us -> none  [per_device(): picked = jnp.sum(ref_masks[:, None, None, None, None, :] * returned, axis=0)]
    unnamed x22 -> x10, local copies, waits for them, and re-layouts: 24 us -> 3.31 us
  transfers between devices with their start and end apart: 6 -> 9, of which waited for: 3 -> 3; matrix products, arithmetic and copies ran while one was open for 12% -> 11% of each run, Pallas kernels for 0% -> 21%
where the time goes in v1:
time: 405 us; the launch traced here: 404 us
  waiting for transfers between devices  174 us (43%)
  Pallas kernels  105 us (26%)
  other arithmetic  42.9 us (11%)
  blocking collectives  30.9 us (8%)
  starting transfers between devices  26.9 us (7%)
  between operations  15.6 us (4%)
  local copies, waits for them, and re-layouts  8.12 us (2%)
    psum x1, waiting for transfers between devices, per_device(): images.append(lax.psum(image, 'freq'))  86.9 us
    pallas_call x2, Pallas kernels, middle(): pl.pallas_call(functools.partial(middle_kernel, outer, sign, rows_n, chun...  61.3 us
    psum x1, waiting for transfers between devices, per_device(): speed = lax.psum(stored, 'freq')  46.7 us
    all_to_all x5, waiting for transfers between devices, per_device(): lax.all_to_all(x, 'space', split_axis=0, concat_axis=0, tiled=True)  40.6 us
    all_to_all x1, blocking collectives, per_device(): lax.all_to_all(x, 'space', split_axis=0, concat_axis=0, tiled=True)  30.9 us
    pallas_call x2, Pallas kernels, final(): pl.pallas_call(functools.partial(final_kernel, outer, chunk, aliased, par...  26.7 us
    all_to_all x5, starting transfers between devices, per_device(): lax.all_to_all(x, 'space', split_axis=0, concat_axis=0, tiled=True)  22.5 us
    pallas_call x2, Pallas kernels, forward_rows(): pl.pallas_call(functools.partial(rows_kernel, outer, cols_n), grid=(rows_...  17.2 us
  transfers between devices with their start and end apart: 9, of which 3 were waited for; matrix products, arithmetic and copies ran while one was open for 11% of the time, Pallas kernels for 21%

profile of v1, /device:TPU:0, one launch (start us, length us, event | category | flops | bytes accessed | tf_op | source)
XLA Modules:
  0.0 403.7 jit_solution(11531289488180241399)
XLA Ops:
  7.2 8.6 %shard_map.214 = f32[8,2,256,256]{3,2,1,0:T(8,128)} custom-call(f32[2,1,2,256,2048]{4,3,2,1,0:T(8,128)} %fields.3, f32[16,2,1,128]{3,2,1,0:T(1,128)} %constant.163.clone.table.refs_7_, bf16[2,256,256]{2,1,0:T(8,128)(2,1)} %constant.164.clone.matrix), custom_call_target="tpu_custom_call" | custom-call | flops 3145728000 | bytes 8388608 | tf_op jit(solution)/shard_map/pallas_call | solution.py:122
  15.7 5.2 %all-to-all-start.2 = ((f32[8,2,256,256]{3,2,1,0:T(8,128)}), f32[8,2,256,256]{3,2,1,0:T(8,128)}, u32[]{:S(2)}, u32[]{:S(2)}) async-start(f32[8,2,256,256]{3,2,1,0:T(8,128)} %shard_map.214), calls=%async_computation.2 | async-start | bytes 8388608 | tf_op jit(solution)/shard_map/all_to_all | solution.py:451
  20.9 8.6 %shard_map.212 = f32[8,2,256,256]{3,2,1,0:T(8,128)} custom-call(f32[2,1,2,256,2048]{4,3,2,1,0:T(8,128)} %fields.3, f32[16,2,1,128]{3,2,1,0:T(1,128)} %constant.163.clone.table.refs_7_, bf16[2,256,256]{2,1,0:T(8,128)(2,1)} %constant.164.clone.matrix), custom_call_target="tpu_custom_call" | custom-call | flops 3145728000 | bytes 8388608 | tf_op jit(solution)/shard_map/pallas_call | solution.py:122
  29.5 40.6 %all-to-all-done.2.refs_1_ = f32[8,2,256,256]{3,2,1,0:T(8,128)} async-done(((f32[8,2,256,256]{3,2,1,0:T(8,128)}), f32[8,2,256,256]{3,2,1,0:T(8,128)}, u32[]{:S(2)}, u32[]{:S(2)}) %all-to-all-start.2) | async-done | bytes 4194336 | tf_op jit(solution)/shard_map/all_to_all | solution.py:451
  70.1 4.7 %all-to-all-start = ((f32[8,2,256,256]{3,2,1,0:T(8,128)}), f32[8,2,256,256]{3,2,1,0:T(8,128)}, u32[]{:S(2)}, u32[]{:S(2)}) async-start(f32[8,2,256,256]{3,2,1,0:T(8,128)} %shard_map.212), calls=%async_computation | async-start | bytes 8388608 | tf_op jit(solution)/shard_map/all_to_all | solution.py:451
  75.9 16.7 %fusion.1 = (f32[2,1,16,128,256]{4,3,2,1,0:T(8,128)S(1)}, f32[2,1,16,128,256]{4,3,2,1,0:T(8,128)S(1)}) fusion(f32[16,128,256]{2,1,0:T(8,128)S(1)} %broadcast_add_fusion, f32[2]{0:T(128)S(1)} %divide_multiply_fusion), kind=kLoop, calls=%fused_computation.7 | loop fusion | flops 7340032 | bytes 10485768 | tf_op jit(solution)/shard_map/jit(_where)/select_n | solution.py:460
  92.6 3.9 pad_maximum_fusion.refs_2_
  96.5 30.6 %shard_map.215 = (f32[8,2,136,256]{3,2,1,0:T(8,128)}, f32[8,2,128,256]{3,2,1,0:T(8,128)}) custom-call(s32[128]{0:T(128)} %bitcast.37, f32[8,2,256,256]{3,2,1,0:T(8,128)} %all-to-all-done.2.refs_1_, f32[2,2,16,128,256]{4,3,2,1,0:T(8,128)} %pad_maximum_fusion.refs_2_, f32[16,2,128,128]{3,2,1,0:T(8,128)} %constant.166.clone.refs_3_, ...), custom_call_target="tpu_custom_call" | custom-call | flops 10485760000 | bytes 16777216 | tf_op jit(solution)/shard_map/pallas_call | solution.py:241
  127.2 30.9 %all_to_all.30.refs_1_ = f32[8,2,128,256]{3,2,1,0:T(8,128)} all-to-all(f32[8,2,128,256]{3,2,1,0:T(8,128)} %get-tuple-element.11), channel_id=1, replica_groups=mesh['freq'=4,'space'=8] {'space'}, dimensions={0} | all-to-all | bytes 4194304 | tf_op jit(solution)/shard_map/all_to_all | solution.py:451
  158.1 3.6 all-to-all-start.5
  162.5 3.1 select_bitcast_fusion
  165.7 0.6 copy-done.4
  166.3 30.7 %shard_map.213 = (f32[8,2,136,256]{3,2,1,0:T(8,128)}, f32[8,2,128,256]{3,2,1,0:T(8,128)}) custom-call(s32[128]{0:T(128)} %bitcast.38, f32[8,2,256,256]{3,2,1,0:T(8,128)} %all-to-all-done.refs_1_, f32[2,2,16,128,256]{4,3,2,1,0:T(8,128)} %pad_maximum_fusion.refs_2_, f32[16,2,128,128]{3,2,1,0:T(8,128)} %constant.166.clone.refs_3_, ...), custom_call_target="tpu_custom_call" | custom-call | flops 10485760000 | bytes 16777216 | tf_op jit(solution)/shard_map/pallas_call | solution.py:241
  197.0 1.4 copy-done.2
  198.4 4.6 %all-to-all-start.4 = ((f32[8,2,136,256]{3,2,1,0:T(8,128)}), f32[8,2,136,256]{3,2,1,0:T(8,128)}, u32[]{:S(2)}, u32[]{:S(2)}) async-start(f32[8,2,136,256]{3,2,1,0:T(8,128)} %get-tuple-element.12), calls=%async_computation.4 | async-start | bytes 4456448 | tf_op jit(solution)/shard_map/all_to_all | solution.py:451
  203.0 1.9 gather_fusion
  204.9 0.6 gather_fusion.1
  205.5 0.6 gather_fusion.2
  206.8 1.2 compare_select_fusion.3
  208.0 46.7 %all-reduce.4.cloned.1.call-done = f32[256,2048]{1,0:T(8,128)} async-done(((f32[256,2048]{1,0:T(8,128)}), f32[256,2048]{1,0:T(8,128)}) %all-reduce.4.cloned.1.call-update) | async-done | bytes 2097168 | tf_op jit(solution)/shard_map/psum | solution.py:449
  254.7 1.0 slice_bitcast_fusion.2
  255.6 1.3 collective-permute-start.1
  256.9 3.0 collective-permute-start
  260.0 4.3 %all-to-all-start.1 = ((f32[8,2,128,256]{3,2,1,0:T(8,128)}), f32[8,2,128,256]{3,2,1,0:T(8,128)S(1)}, u32[]{:S(2)}, u32[]{:S(2)}) async-start(f32[8,2,128,256]{3,2,1,0:T(8,128)} %get-tuple-element.10), calls=%async_computation.1 | async-start | bytes 4194304 | tf_op jit(solution)/shard_map/all_to_all | solution.py:451
  264.4 11.1 %multiply_bitcast_fusion.1 = (f32[1,256,2048]{2,1,0:T(8,128)S(1)}, f32[1,256,2048]{2,1,0:T(8,128)S(1)}, f32[256,2048]{1,0:T(8,128)}) fusion(f32[256]{0:T(256)S(1)} %get-tuple-element.39, f32[256]{0:T(256)S(1)} %get-tuple-element.35, f32[256,2048]{1,0:T(8,128)} %all-reduce.4.cloned.1.call-done, pred[256]{0:T(512)(128)(4,1)S(1)} %get-tuple-element.38, ...), kind=kLoop, calls=%fused_computation.18 | loop fusion | flops 4718592 | bytes 8392968 | tf_op jit(solution)/shard_map/stack | solution.py:489
  275.4 2.3 pad_maximum_fusion.1.refs_4_
  278.2 0.7 pad_maximum_fusion.2.refs_5_
  278.9 13.3 %shard_map.216 = (f32[2,1,2,256,2048]{4,3,2,1,0:T(8,128)}, f32[128,2048]{1,0:T(8,128)}) custom-call(f32[8,2,136,256]{3,2,1,0:T(8,128)} %all-to-all-done.4.refs_0_.refs_2_, f32[8,2,136,256]{3,2,1,0:T(8,128)} %copy-done.2, f32[8,2,136,256]{3,2,1,0:T(8,128)} %all-to-all-done.4.refs_0_.refs_2_, f32[8,2,136,256]{3,2,1,0:T(8,128)} %copy-done.2, ...), custom_call_target="tpu_custom_call" | custom-call | flops 3932160000 | bytes 15728640 | tf_op jit(solution)/shard_map/pallas_call | solution.py:381
  292.2 1.3 copy-done.3
  293.5 13.4 %shard_map.217 = (f32[2,1,2,256,2048]{4,3,2,1,0:T(8,128)}, f32[128,2048]{1,0:T(8,128)}) custom-call(f32[8,2,128,256]{3,2,1,0:T(8,128)} %copy-done.3, f32[8,2,128,256]{3,2,1,0:T(8,128)} %all_to_all.30.refs_1_, f32[8,2,136,256]{3,2,1,0:T(8,128)} %all-to-all-done.4.refs_0_.refs_2_, f32[8,2,136,256]{3,2,1,0:T(8,128)} %copy-done.2, ...), custom_call_target="tpu_custom_call", output_to_operand_aliasing={{0}: (9, {})} | custom-call | flops 3932160000 | bytes 15728640 | tf_op jit(solution)/shard_map/pallas_call | solution.py:381
  306.9 86.9 %all-reduce.6.cloned.1.call-done = (f32[128,2048]{1,0:T(8,128)}, f32[128,2048]{1,0:T(8,128)}) async-done(((f32[128,2048]{1,0:T(8,128)}, f32[128,2048]{1,0:T(8,128)}), (f32[128,2048]{1,0:T(8,128)}, f32[128,2048]{1,0:T(8,128)})) %all-reduce.6.cloned.1.call-update) | async-done | bytes 2097168 | tf_op jit(solution)/shard_map/psum | solution.py:505
  393.8 3.1 maximum_bitcast_fusion
  (34 shorter events, 1.6 us)
Async XLA Ops:
  15.7 54.4 %all-to-all-start.2 = ((f32[8,2,256,256]{3,2,1,0:T(8,128)}), f32[8,2,256,256]{3,2,1,0:T(8,128)}, u32[]{:S(2)}, u32[]{:S(2)}) async-start(f32[8,2,256,256]{3,2,1,0:T(8,128)} %shard_map.214), calls=%async_computation.2 | async-start | bytes 8388608 | tf_op jit(solution)/shard_map/all_to_all | solution.py:451
  29.5 46.1 %copy-start.1 = (f32[1,2]{1,0:T(1,128)S(1)}, f32[1,2]{1,0:T(1,128)}, u32[]{:S(2)}) copy-start(f32[1,2]{1,0:T(1,128)} %param.25) | copy-start | bytes 28
  70.1 57.1 %all-to-all-start = ((f32[8,2,256,256]{3,2,1,0:T(8,128)}), f32[8,2,256,256]{3,2,1,0:T(8,128)}, u32[]{:S(2)}, u32[]{:S(2)}) async-start(f32[8,2,256,256]{3,2,1,0:T(8,128)} %shard_map.212), calls=%async_computation | async-start | bytes 8388608 | tf_op jit(solution)/shard_map/all_to_all | solution.py:451
  158.1 38.8 %all-to-all-start.5 = ((f32[8,2,136,256]{3,2,1,0:T(8,128)}), f32[8,2,136,256]{3,2,1,0:T(8,128)S(1)}, u32[]{:S(2)}, u32[]{:S(2)}) async-start(f32[8,2,136,256]{3,2,1,0:T(8,128)} %get-tuple-element.13), calls=%async_computation.5 | async-start | bytes 4456448 | tf_op jit(solution)/shard_map/all_to_all | solution.py:451
  161.7 92.9 %all-reduce.4.cloned.1.call-start = ((), (), s32[]{:S(2)}) async-start(), calls=%async_computation.6 | async-start | bytes 4194304 | tf_op jit(solution)/shard_map/psum | solution.py:449
  165.6 0.7 copy-start.4
  196.9 1.4 copy-start.2
  197.0 6.0 %copy-start = (s32[1,128]{1,0:T(1,128)S(1)}, s32[1,128]{1,0:T(1,128)}, u32[]{:S(2)}) copy-start(s32[1,128]{1,0:T(1,128)} %param.26) | copy-start | bytes 1540
  198.4 61.6 %all-to-all-start.4 = ((f32[8,2,136,256]{3,2,1,0:T(8,128)}), f32[8,2,136,256]{3,2,1,0:T(8,128)}, u32[]{:S(2)}, u32[]{:S(2)}) async-start(f32[8,2,136,256]{3,2,1,0:T(8,128)} %get-tuple-element.12), calls=%async_computation.4 | async-start | bytes 4456448 | tf_op jit(solution)/shard_map/all_to_all | solution.py:451
  255.6 22.1 %collective-permute-start.1 = (f32[1,2048]{1,0:T(1,128)S(1)}, f32[1,2048]{1,0:T(1,128)S(1)}, u32[]{:S(2)}, u32[]{:S(2)}) collective-permute-start(f32[1,2048]{1,0:T(1,128)S(1)} %get-tuple-element.28), channel_id=1, source_target_pairs={{1,0},{2,1},{3,2},{4,3},{5,4},{6,5},{7,6},{9,8},{10,9},{11,10},{12... | collective-permute-start | bytes 24584 | tf_op jit(solution)/shard_map/ppermute | solution.py:468
  256.9 20.8 %collective-permute-start = (f32[1,2048]{1,0:T(1,128)S(1)}, f32[1,2048]{1,0:T(1,128)S(1)}, u32[]{:S(2)}, u32[]{:S(2)}) collective-permute-start(f32[1,2048]{1,0:T(1,128)S(1)} %get-tuple-element.31), channel_id=1, source_target_pairs={{0,1},{1,2},{2,3},{3,4},{4,5},{5,6},{6,7},{8,9},{9,10},{10,11},{11... | collective-permute-start | bytes 24584 | tf_op jit(solution)/shard_map/ppermute | solution.py:467
  260.0 32.2 %all-to-all-start.1 = ((f32[8,2,128,256]{3,2,1,0:T(8,128)}), f32[8,2,128,256]{3,2,1,0:T(8,128)S(1)}, u32[]{:S(2)}, u32[]{:S(2)}) async-start(f32[8,2,128,256]{3,2,1,0:T(8,128)} %get-tuple-element.10), calls=%async_computation.1 | async-start | bytes 4194304 | tf_op jit(solution)/shard_map/all_to_all | solution.py:451
  264.3 129.5 %all-reduce.6.cloned.1.call-start = ((), (), s32[]{:S(2)}) async-start(), calls=%async_computation.7 | async-start | bytes 4194304 | tf_op jit(solution)/shard_map/psum | solution.py:505
  292.2 1.3 copy-start.3
Sparse Core Ops, SparseCore 0:
  165.7 88.8 all-reduce.3
  307.0 86.7 all-reduce.5

commit v2 on v1

--- a/solution.py
+++ b/solution.py
@@ -446,10 +446,13 @@
     owner = slab_owner[0]
     stored = lax.dynamic_index_in_dim(velocity, owner % slab_local, 0, keepdims=False)
     stored = jnp.where(lax.axis_index("freq") == owner // slab_local, stored, 0.0)
+    first = forward_rows(wavefields, 0, space, cols_n)
+    first, stored = lax.optimization_barrier((first, stored))
     speed = lax.psum(stored, "freq")
 
     swap = lambda x: lax.all_to_all(x, "space", split_axis=0, concat_axis=0, tiled=True)
-    spectra = [swap(forward_rows(wavefields, j, space, cols_n)) for j in range(2)]
+    spectra = [swap(first), swap(forward_rows(wavefields, 1, space, cols_n))]
+    spectra[1], speed = lax.optimization_barrier((spectra[1], speed))
 
     ky = wave_values(me * cols_n + jnp.arange(cols_n, dtype=jnp.int32), width_y)
     kx = wave_values(jnp.arange(width_x, dtype=jnp.int32), width_x)
@@ -498,11 +501,27 @@
     moved = []
     for j in range(2):
         moved.append(middle(spectra[j], phase, block_refs, -1.0 if j == 0 else 1.0, chunks))
-    back = [[swap(moved[j][h]) for j in range(2)] for h in range(chunks)]
+    back, latest = [], None
+    for h in range(chunks):
+        row = []
+        for j in range(2):
+            sent = moved[j][h]
+            if h:
+                sent, latest = lax.optimization_barrier((sent, latest))
+                if j == 0:
+                    back[-1][1] = latest
+                else:
+                    row[0] = latest
+            latest = swap(sent)
+            row.append(latest)
+        back.append(row)
     fields, images = None, []
     for h in range(chunks):
         fields, image = final(back[h], back[0], shift, shift_edge, beta, h, chunks, fields)
-        images.append(lax.psum(image, "freq"))
+        if h + 1 < chunks:
+            images.append(jnp.sum(lax.all_gather(image, "freq"), axis=0))
+        else:
+            images.append(lax.psum(image, "freq"))
     return fields, jnp.concatenate(images, axis=0)[None]
 
 

time: 405 us -> 424 us (1.047)
  blocking collectives: 30.9 us -> 60.8 us
  waiting for transfers between devices: 174 us -> 168 us
    psum x1, waiting for transfers between devices: 86.9 us -> 50.9 us  [per_device(): images.append(lax.psum(image, 'freq'))]
    all_to_all x1 -> x2, blocking collectives: 30.9 us -> 60.8 us  [per_device(): lax.all_to_all(x, 'space', split_axis=0, concat_axis=0, tiled=True)]
    psum x1, waiting for transfers between devices: 46.7 us -> 66.5 us  [per_device(): speed = lax.psum(stored, 'freq')]
    all_gather x0 -> x1, waiting for transfers between devices: none -> 4.76 us  [per_device(): images.append(jnp.sum(lax.all_gather(image, 'freq'), axis=0))]
    all_to_all x5 -> x4, waiting for transfers between devices: 40.6 us -> 45.1 us  [per_device(): lax.all_to_all(x, 'space', split_axis=0, concat_axis=0, tiled=True)]
    all_to_all x5 -> x4, starting transfers between devices: 22.5 us -> 18 us  [per_device(): lax.all_to_all(x, 'space', split_axis=0, concat_axis=0, tiled=True)]
  transfers between devices with their start and end apart: 9 -> 9, of which waited for: 3 -> 5; matrix products, arithmetic and copies ran while one was open for 11% -> 11% of each run, Pallas kernels for 21% -> 20%
where the time goes in v2:
time: 424 us; the launch traced here: 423 us
  waiting for transfers between devices  168 us (40%)
  Pallas kernels  105 us (25%)
  blocking collectives  60.8 us (14%)
  other arithmetic  45.1 us (11%)
  starting transfers between devices  22.7 us (5%)
  between operations  15.3 us (4%)
  local copies, waits for them, and re-layouts  6.25 us (1%)
    psum x1, waiting for transfers between devices, per_device(): speed = lax.psum(stored, 'freq')  66.5 us
    pallas_call x2, Pallas kernels, middle(): pl.pallas_call(functools.partial(middle_kernel, outer, sign, rows_n, chun...  61.4 us
    all_to_all x2, blocking collectives, per_device(): lax.all_to_all(x, 'space', split_axis=0, concat_axis=0, tiled=True)  60.8 us
    psum x1, waiting for transfers between devices, per_device(): images.append(lax.psum(image, 'freq'))  50.9 us
    all_to_all x4, waiting for transfers between devices, per_device(): lax.all_to_all(x, 'space', split_axis=0, concat_axis=0, tiled=True)  45.1 us
    pallas_call x2, Pallas kernels, final(): pl.pallas_call(functools.partial(final_kernel, outer, chunk, aliased, par...  26.6 us
    all_to_all x4, starting transfers between devices, per_device(): lax.all_to_all(x, 'space', split_axis=0, concat_axis=0, tiled=True)  18 us
    pallas_call x2, Pallas kernels, forward_rows(): pl.pallas_call(functools.partial(rows_kernel, outer, cols_n), grid=(rows_...  17.1 us
  transfers between devices with their start and end apart: 9, of which 5 were waited for; matrix products, arithmetic and copies ran while one was open for 11% of the time, Pallas kernels for 20%

profile of v2, /device:TPU:0, one launch (start us, length us, event | category | flops | bytes accessed | tf_op | source)
XLA Modules:
  0.0 423.0 jit_solution(2445801353098273505)
XLA Ops:
  7.2 8.6 %shard_map.212 = f32[8,2,256,256]{3,2,1,0:T(8,128)} custom-call(f32[2,1,2,256,2048]{4,3,2,1,0:T(8,128)} %fields.3, f32[16,2,1,128]{3,2,1,0:T(1,128)} %constant.163.clone.table.refs_7_, bf16[2,256,256]{2,1,0:T(8,128)(2,1)} %constant.164.clone.matrix), custom_call_target="tpu_custom_call" | custom-call | flops 3145728000 | bytes 8388608 | tf_op jit(solution)/shard_map/pallas_call | solution.py:122
  15.7 5.2 %all-to-all-start = ((f32[8,2,256,256]{3,2,1,0:T(8,128)}), f32[8,2,256,256]{3,2,1,0:T(8,128)}, u32[]{:S(2)}, u32[]{:S(2)}) async-start(f32[8,2,256,256]{3,2,1,0:T(8,128)} %shard_map.212), calls=%async_computation | async-start | bytes 8388608 | tf_op jit(solution)/shard_map/all_to_all | solution.py:453
  21.6 3.1 select_bitcast_fusion
  24.7 8.5 %shard_map.213 = f32[8,2,256,256]{3,2,1,0:T(8,128)} custom-call(f32[2,1,2,256,2048]{4,3,2,1,0:T(8,128)} %fields.3, f32[16,2,1,128]{3,2,1,0:T(1,128)} %constant.163.clone.table.refs_7_, bf16[2,256,256]{2,1,0:T(8,128)(2,1)} %constant.164.clone.matrix), custom_call_target="tpu_custom_call" | custom-call | flops 3145728000 | bytes 8388608 | tf_op jit(solution)/shard_map/pallas_call | solution.py:122
  33.3 36.9 %all-to-all-done.refs_1_ = f32[8,2,256,256]{3,2,1,0:T(8,128)} async-done(((f32[8,2,256,256]{3,2,1,0:T(8,128)}), f32[8,2,256,256]{3,2,1,0:T(8,128)}, u32[]{:S(2)}, u32[]{:S(2)}) %all-to-all-start) | async-done | bytes 4194336 | tf_op jit(solution)/shard_map/all_to_all | solution.py:453
  70.1 4.6 %all-to-all-start.1 = ((f32[8,2,256,256]{3,2,1,0:T(8,128)}), f32[8,2,256,256]{3,2,1,0:T(8,128)}, u32[]{:S(2)}, u32[]{:S(2)}) async-start(f32[8,2,256,256]{3,2,1,0:T(8,128)} %shard_map.213), calls=%async_computation.1 | async-start | bytes 8388608 | tf_op jit(solution)/shard_map/all_to_all | solution.py:453
  76.2 1.9 gather_fusion
  78.1 0.6 gather_fusion.1
  80.4 16.7 %fusion.1 = (f32[2,1,16,128,256]{4,3,2,1,0:T(8,128)S(1)}, f32[2,1,16,128,256]{4,3,2,1,0:T(8,128)S(1)}) fusion(f32[16,128,256]{2,1,0:T(8,128)S(1)} %broadcast_add_fusion, f32[2]{0:T(128)S(1)} %divide_multiply_fusion), kind=kLoop, calls=%fused_computation.7 | loop fusion | flops 7340032 | bytes 10485768 | tf_op jit(solution)/shard_map/jit(_where)/select_n | solution.py:463
  97.1 3.9 pad_maximum_fusion.refs_2_
  101.0 66.5 %all-reduce.3.cloned.1.call-done = f32[256,2048]{1,0:T(8,128)} async-done(((f32[256,2048]{1,0:T(8,128)}), f32[256,2048]{1,0:T(8,128)}) %all-reduce.3.cloned.1.call-update) | async-done | bytes 2097168 | tf_op jit(solution)/shard_map/psum | solution.py:451
  167.5 30.8 %shard_map.214 = (f32[8,2,136,256]{3,2,1,0:T(8,128)}, f32[8,2,128,256]{3,2,1,0:T(8,128)}) custom-call(s32[128]{0:T(128)} %bitcast.38, f32[8,2,256,256]{3,2,1,0:T(8,128)} %all-to-all-done.refs_1_, f32[2,2,16,128,256]{4,3,2,1,0:T(8,128)} %pad_maximum_fusion.refs_2_, f32[16,2,128,128]{3,2,1,0:T(8,128)} %constant.166.clone.refs_3_, ...), custom_call_target="tpu_custom_call" | custom-call | flops 10485760000 | bytes 16777216 | tf_op jit(solution)/shard_map/pallas_call | solution.py:241
  198.3 3.7 all-to-all-start.2
  202.0 1.2 compare_select_fusion.3
  203.3 30.6 %shard_map.215 = (f32[8,2,136,256]{3,2,1,0:T(8,128)}, f32[8,2,128,256]{3,2,1,0:T(8,128)}) custom-call(s32[128]{0:T(128)} %bitcast.39, f32[8,2,256,256]{3,2,1,0:T(8,128)} %all-to-all-done.1.refs_1_, f32[2,2,16,128,256]{4,3,2,1,0:T(8,128)} %pad_maximum_fusion.refs_2_, f32[16,2,128,128]{3,2,1,0:T(8,128)} %constant.166.clone.refs_3_, ...), custom_call_target="tpu_custom_call" | custom-call | flops 10485760000 | bytes 16777216 | tf_op jit(solution)/shard_map/pallas_call | solution.py:241
  233.9 1.4 copy-done.2
  235.3 4.6 %all-to-all-start.5 = ((f32[8,2,136,256]{3,2,1,0:T(8,128)}), f32[8,2,136,256]{3,2,1,0:T(8,128)}, u32[]{:S(2)}, u32[]{:S(2)}) async-start(f32[8,2,136,256]{3,2,1,0:T(8,128)} %get-tuple-element.27), calls=%async_computation.5 | async-start | bytes 4456448 | tf_op jit(solution)/shard_map/all_to_all | solution.py:453
  240.0 1.0 slice_bitcast_fusion.2
  240.9 1.3 collective-permute-start.1
  242.2 3.0 collective-permute-start
  245.3 11.1 %multiply_bitcast_fusion.1 = (f32[1,256,2048]{2,1,0:T(8,128)S(1)}, f32[1,256,2048]{2,1,0:T(8,128)S(1)}, f32[256,2048]{1,0:T(8,128)}) fusion(f32[256]{0:T(256)S(1)} %get-tuple-element.53, f32[256]{0:T(256)S(1)} %get-tuple-element.49, f32[256,2048]{1,0:T(8,128)} %all-reduce.3.cloned.1.call-done, pred[256]{0:T(512)(128)(4,1)S(1)} %get-tuple-element.52, ...), kind=kLoop, calls=%fused_computation.18 | loop fusion | flops 4718592 | bytes 8392968 | tf_op jit(solution)/shard_map/stack | solution.py:492
  256.3 2.3 pad_maximum_fusion.1.refs_4_
  259.1 0.7 pad_maximum_fusion.2.refs_5_
  259.7 8.2 %all-to-all-done.5.refs_0_.refs_2_ = f32[8,2,136,256]{3,2,1,0:T(8,128)} async-done(((f32[8,2,136,256]{3,2,1,0:T(8,128)}), f32[8,2,136,256]{3,2,1,0:T(8,128)}, u32[]{:S(2)}, u32[]{:S(2)}) %all-to-all-start.5) | async-done | bytes 2228256 | tf_op jit(solution)/shard_map/all_to_all | solution.py:453
  268.0 13.3 %shard_map.216 = (f32[2,1,2,256,2048]{4,3,2,1,0:T(8,128)}, f32[128,2048]{1,0:T(8,128)}) custom-call(f32[8,2,136,256]{3,2,1,0:T(8,128)} %all-to-all-done.5.refs_0_.refs_2_, f32[8,2,136,256]{3,2,1,0:T(8,128)} %copy-done.2, f32[8,2,136,256]{3,2,1,0:T(8,128)} %all-to-all-done.5.refs_0_.refs_2_, f32[8,2,136,256]{3,2,1,0:T(8,128)} %copy-done.2, ...), custom_call_target="tpu_custom_call" | custom-call | flops 3932160000 | bytes 15728640 | tf_op jit(solution)/shard_map/pallas_call | solution.py:381
  281.4 31.1 %all_to_all.30.refs_0_ = f32[8,2,128,256]{3,2,1,0:T(8,128)} all-to-all(f32[8,2,128,256]{3,2,1,0:T(8,128)} %get-tuple-element.24), channel_id=1, replica_groups=mesh['freq'=4,'space'=8] {'space'}, dimensions={0} | all-to-all | bytes 4194304 | tf_op jit(solution)/shard_map/all_to_all | solution.py:453
  312.4 29.7 %all_to_all.31.refs_1_ = f32[8,2,128,256]{3,2,1,0:T(8,128)} all-to-all(f32[8,2,128,256]{3,2,1,0:T(8,128)S(1)} %copy-done.3), channel_id=1, replica_groups=mesh['freq'=4,'space'=8] {'space'}, dimensions={0} | all-to-all | bytes 4194304 | tf_op jit(solution)/shard_map/all_to_all | solution.py:453
  342.2 13.3 %shard_map.217 = (f32[2,1,2,256,2048]{4,3,2,1,0:T(8,128)}, f32[128,2048]{1,0:T(8,128)}) custom-call(f32[8,2,128,256]{3,2,1,0:T(8,128)} %all_to_all.30.refs_0_, f32[8,2,128,256]{3,2,1,0:T(8,128)} %all_to_all.31.refs_1_, f32[8,2,136,256]{3,2,1,0:T(8,128)} %all-to-all-done.5.refs_0_.refs_2_, ...), custom_call_target="tpu_custom_call", output_to_operand_aliasing={{0}: (9, {})} | custom-call | flops 3932160000 | bytes 15728640 | tf_op jit(solution)/shard_map/pallas_call | solution.py:381
  355.5 4.8 %all-gather.3.cloned.1.call-done = f32[512,2048]{1,0:T(8,128)} async-done(((f32[128,2048]{1,0:T(8,128)}), f32[512,2048]{1,0:T(8,128)}) %all-gather.3.cloned.1.call-update) | async-done | bytes 4194320 | tf_op jit(solution)/shard_map/all_gather | solution.py:522
  360.3 2.6 reduce_sum.9
  362.9 50.9 %all-reduce.5.cloned.1.call-done = f32[128,2048]{1,0:T(8,128)} async-done(((f32[128,2048]{1,0:T(8,128)}), f32[128,2048]{1,0:T(8,128)}) %all-reduce.5.cloned.1.call-update) | async-done | bytes 1048592 | tf_op jit(solution)/shard_map/psum | solution.py:524
  413.7 2.7 maximum_bitcast_fusion
  (37 shorter events, 3.0 us)
Async XLA Ops:
  15.7 54.4 %all-to-all-start = ((f32[8,2,256,256]{3,2,1,0:T(8,128)}), f32[8,2,256,256]{3,2,1,0:T(8,128)}, u32[]{:S(2)}, u32[]{:S(2)}) async-start(f32[8,2,256,256]{3,2,1,0:T(8,128)} %shard_map.212), calls=%async_computation | async-start | bytes 8388608 | tf_op jit(solution)/shard_map/all_to_all | solution.py:453
  70.1 128.2 %all-to-all-start.1 = ((f32[8,2,256,256]{3,2,1,0:T(8,128)}), f32[8,2,256,256]{3,2,1,0:T(8,128)}, u32[]{:S(2)}, u32[]{:S(2)}) async-start(f32[8,2,256,256]{3,2,1,0:T(8,128)} %shard_map.213), calls=%async_computation.1 | async-start | bytes 8388608 | tf_op jit(solution)/shard_map/all_to_all | solution.py:453
  74.7 1.5 copy-start
  74.7 3.3 copy-start.4
  74.7 4.0 copy-start.1
  74.7 92.7 %all-reduce.3.cloned.1.call-start = ((), (), s32[]{:S(2)}) async-start(), calls=%async_computation.6 | async-start | bytes 4194304 | tf_op jit(solution)/shard_map/psum | solution.py:451
  198.3 35.6 %all-to-all-start.2 = ((f32[8,2,136,256]{3,2,1,0:T(8,128)}), f32[8,2,136,256]{3,2,1,0:T(8,128)S(1)}, u32[]{:S(2)}, u32[]{:S(2)}) async-start(f32[8,2,136,256]{3,2,1,0:T(8,128)} %get-tuple-element.23), calls=%async_computation.2 | async-start | bytes 4456448 | tf_op jit(solution)/shard_map/all_to_all | solution.py:453
  233.9 1.4 copy-start.2
  235.3 32.7 %all-to-all-start.5 = ((f32[8,2,136,256]{3,2,1,0:T(8,128)}), f32[8,2,136,256]{3,2,1,0:T(8,128)}, u32[]{:S(2)}, u32[]{:S(2)}) async-start(f32[8,2,136,256]{3,2,1,0:T(8,128)} %get-tuple-element.27), calls=%async_computation.5 | async-start | bytes 4456448 | tf_op jit(solution)/shard_map/all_to_all | solution.py:453
  239.9 120.4 %all-gather.3.cloned.1.call-start = ((), (), s32[]{:S(2)}) async-start(), calls=%async_computation.8 | async-start | bytes 5242880 | tf_op jit(solution)/shard_map/all_gather | solution.py:522
  240.9 17.7 %collective-permute-start.1 = (f32[1,2048]{1,0:T(1,128)S(1)}, f32[1,2048]{1,0:T(1,128)S(1)}, u32[]{:S(2)}, u32[]{:S(2)}) collective-permute-start(f32[1,2048]{1,0:T(1,128)S(1)} %get-tuple-element.42), channel_id=1, source_target_pairs={{1,0},{2,1},{3,2},{4,3},{5,4},{6,5},{7,6},{9,8},{10,9},{11,10},{12... | collective-permute-start | bytes 24584 | tf_op jit(solution)/shard_map/ppermute | solution.py:471
  242.2 16.4 %collective-permute-start = (f32[1,2048]{1,0:T(1,128)S(1)}, f32[1,2048]{1,0:T(1,128)S(1)}, u32[]{:S(2)}, u32[]{:S(2)}) collective-permute-start(f32[1,2048]{1,0:T(1,128)S(1)} %get-tuple-element.45), channel_id=1, source_target_pairs={{0,1},{1,2},{2,3},{3,4},{4,5},{5,6},{6,7},{8,9},{9,10},{10,11},{11... | collective-permute-start | bytes 24584 | tf_op jit(solution)/shard_map/ppermute | solution.py:470
  281.3 31.1 %copy-start.3 = (f32[8,2,128,256]{3,2,1,0:T(8,128)S(1)}, f32[8,2,128,256]{3,2,1,0:T(8,128)}, u32[]{:S(2)}) copy-start(f32[8,2,128,256]{3,2,1,0:T(8,128)} %get-tuple-element.26) | copy-start | bytes 6291460
  281.3 132.4 %all-reduce.5.cloned.1.call-start = ((), (), s32[]{:S(2)}) async-start(), calls=%async_computation.7 | async-start | bytes 2097152 | tf_op jit(solution)/shard_map/psum | solution.py:524
Sparse Core Ops, SparseCore 0:
  78.5 88.9 all-reduce.2
  281.4 78.8 all-gather.2
  363.4 50.3 all-reduce.4
